TPU v7x, 32 devices: a whole 2x2x4 slice. The times are simulated.
32 devices in a mesh: ctx: 8 (over z, y), head: 4 (over x, core).
Axes of the slice: x: 2, y: 2, z: 4, core: 2. Of those that a mesh axis runs over, the one named last changes fastest.
Arguments:
- queries: bfloat16 [1024, 2048], P('ctx', 'head'), may hold values from -6 to 6
- keys: bfloat16 [1024, 2048], P('ctx', 'head'), may hold values from -6 to 6
- values: bfloat16 [1024, 4096], P('ctx', 'head'), may hold values from -6 to 6
- out_gate: bfloat16 [1024, 4096], P('ctx', 'head'), may hold values from -6 to 6
- log_decay: float32 [1024, 32], P('ctx', 'head'), may hold values from -1.5 to 0, as said below
- write_strength: float32 [1024, 32], P('ctx', 'head'), may hold values from 0 to 1
- segment_ids: int32 [1024], P('ctx'), may hold values from 0 to 2, never falling along the last dimension, each value on 1 to 512 neighbouring positions
- head_order: int32 [32], replicated, may hold values from 0 to 31, each once
- out_weight: bfloat16 [4096, 2048], P('head'), may hold values from -0.09375 to 0.09375
Outputs:
- layer_out: bfloat16 [1024, 2048], P(('ctx', 'head'))
- decode_states: float32 [32, 16384], P('head', 'ctx')
Inputs may be any that keep to these rules, and one draw needn't show every extreme that they name: `log_decay`: Negative.
All inputs are finite; a program needn't handle non-finite values.
Results may differ from a plain program's by a relative error of at most 0.0049.
Values may be sent and summed in bfloat16 or wider, within the bound.
A program may use at most 192 MiB of HBM per device.

v0:
```python
import jax
import jax.numpy as jnp
from jax import lax
from jax.sharding import PartitionSpec as P

DK = 128
DV = 128
BLOCK = 64


highest = lax.Precision.HIGHEST
norm_eps = 1e-06


def prefix(x, axis, combine, identity):
    peers, index = (lax.axis_size(axis), lax.axis_index(axis))
    everything = jax.tree.map(lambda part: lax.all_gather(part, axis), x)
    start = jax.tree.map(
        lambda part, zero: jnp.broadcast_to(jnp.asarray(zero, part.dtype), part.shape), x, identity
    )

    def step(k, before):
        reached = k < index
        new = combine(before, jax.tree.map(lambda part: part[k], everything))
        return jax.tree.map(lambda a, b: jnp.where(reached, a, b), new, before)

    return lax.fori_loop(0, peers, step, start)


def product(form, left, right):
    return jnp.einsum(form, left, right, precision=highest)


def unit_rows(raw_rows, scaling):
    widened = raw_rows.astype(jnp.float32)
    return (
        widened * lax.rsqrt(jnp.sum(widened * widened, axis=-1, keepdims=True) + norm_eps) * scaling
    )


def gated_norm(attention, gate_rows):
    mean_square = jnp.mean(attention * attention, axis=-1, keepdims=True)
    gated = (
        attention * lax.rsqrt(mean_square + norm_eps) * jax.nn.silu(gate_rows.astype(jnp.float32))
    )
    return gated.astype(jnp.bfloat16)


def inverse_unit_lower(coupling):
    block_size = coupling.shape[-1]
    identity_matrix = jnp.eye(block_size, dtype=jnp.float32)
    inverse = identity_matrix - coupling
    squared = coupling
    for doubling in range(block_size.bit_length() - 2):
        squared = product("...ij,...jk->...ik", squared, squared)
        inverse = product("...ij,...jk->...ik", inverse, identity_matrix + squared)
    return inverse


def block_parts(query_part, key_part, value_part, decay_rows, strength_rows, doc_rows, doc_before):
    block_size = doc_rows.shape[-1]
    token_positions = jnp.arange(block_size)
    causal = token_positions[:, None] >= token_positions[None, :]
    strict = token_positions[:, None] > token_positions[None, :]
    same_doc = (doc_rows[..., :, None] == doc_rows[..., None, :]) & causal
    continues = doc_rows == doc_before[..., None]
    cumulative = jnp.cumsum(decay_rows, axis=-1)
    decay_gap = cumulative[..., :, None] - cumulative[..., None, :]
    mixing = jnp.where(same_doc[..., None, :, :], jnp.exp(jnp.minimum(decay_gap, 0.0)), 0.0)
    entry_decay = jnp.where(continues[..., None, :], jnp.exp(cumulative), 0.0)
    key_intersection = product("...id,...jd->...ij", key_part, key_part)
    coupling = jnp.where(strict, strength_rows[..., :, None] * mixing * key_intersection, 0.0)
    inverse = inverse_unit_lower(coupling)
    weighted = product(
        "...ij,...jd->...id", inverse, (strength_rows * entry_decay)[..., None] * key_part
    )
    pseudo_values = product("...ij,...jd->...id", inverse, strength_rows[..., None] * value_part)
    masked_scores = mixing * product("...id,...jd->...ij", query_part, key_part)
    local_out = product("...ij,...jd->...id", masked_scores, pseudo_values)
    state_read = entry_decay[..., None] * query_part - product(
        "...ij,...jd->...id", masked_scores, weighted
    )
    last_keys = mixing[..., -1, :, None] * key_part
    identity_map = jnp.eye(key_part.shape[-1], dtype=jnp.float32)
    transition = entry_decay[..., -1, None, None] * identity_map - product(
        "...jd,...je->...de", last_keys, weighted
    )
    written = product("...jd,...je->...de", last_keys, pseudo_values)
    return (local_out, state_read, transition, written)


def combine_spans(earlier, later):
    linked = jnp.where((earlier[3] < 0) | (later[2] < 0) | (earlier[3] == later[2]), 1.0, 0.0)
    through = linked * product("hde,hef->hdf", later[0], earlier[0])
    reached = linked * product("hde,hef->hdf", later[0], earlier[1]) + later[1]
    first_doc = jnp.where(earlier[2] >= 0, earlier[2], later[2])
    last_doc = jnp.where(later[3] >= 0, later[3], earlier[3])
    return (through, reached, first_doc, last_doc)


def per_device(
    queries, keys, values, out_gate, log_decay, write_strength, segment_ids, head_order, out_weight
):
    tok_rows = queries.shape[0]
    heads_here = values.shape[1] // DV
    key_groups = queries.shape[1] // DK
    group_size = heads_here // key_groups
    blocks = tok_rows // BLOCK

    def head_major(raw_rows, scaling):
        unit_part = unit_rows(raw_rows.reshape(blocks, BLOCK, key_groups, DK), scaling)
        return jnp.repeat(unit_part, group_size, axis=2).transpose(0, 2, 1, 3)

    query_part = head_major(queries, DK ** (-0.5))
    key_part = head_major(keys, 1.0)
    value_part = (
        values.reshape(blocks, BLOCK, heads_here, DV).astype(jnp.float32).transpose(0, 2, 1, 3)
    )
    decay_rows = log_decay.reshape(blocks, BLOCK, heads_here).transpose(0, 2, 1)
    strength_rows = write_strength.reshape(blocks, BLOCK, heads_here).transpose(0, 2, 1)
    doc_blocks = segment_ids.reshape(blocks, BLOCK)
    doc_before = jnp.concatenate([doc_blocks[:1, 0], doc_blocks[:-1, -1]])
    local_out, state_read, transition, written = block_parts(
        query_part, key_part, value_part, decay_rows, strength_rows, doc_blocks, doc_before
    )
    identity_map = jnp.broadcast_to(jnp.eye(DK, dtype=jnp.float32), (heads_here, DK, DK))
    zero_state = jnp.zeros((heads_here, DK, DV), jnp.float32)

    def compose_keep(carried, pieces):
        through, reached = carried
        step_map, step_add = pieces
        updated = (
            product("hde,hef->hdf", step_map, through),
            product("hde,hef->hdf", step_map, reached) + step_add,
        )
        return (updated, carried)

    (whole_map, whole_add), (prefix_maps, prefix_states) = lax.scan(
        compose_keep, (identity_map, zero_state), (transition, written)
    )
    early_out = local_out + product("chid,chde->chie", state_read, prefix_states)
    first_doc = doc_blocks[0, 0].astype(jnp.float32)
    last_doc = doc_blocks[-1, -1].astype(jnp.float32)
    identity = (identity_map, zero_state, jnp.float32(-1.0), jnp.float32(-1.0))
    before = prefix((whole_map, whole_add, first_doc, last_doc), "ctx", combine_spans, identity)
    linked = jnp.where((before[3] < 0) | (before[3] == first_doc), 1.0, 0.0)
    incoming = linked * before[1]
    reach = product("chde,hef->chdf", prefix_maps, incoming)
    attention = early_out + product("chid,chde->chie", state_read, reach)
    final_state = product("hde,hef->hdf", whole_map, incoming) + whole_add
    tokens_major = attention.transpose(0, 2, 1, 3).reshape(tok_rows, heads_here, DV)
    normed = gated_norm(tokens_major, out_gate.reshape(tok_rows, heads_here, DV)).reshape(
        tok_rows, heads_here * DV
    )
    summed = lax.psum_scatter(
        jnp.dot(normed, out_weight, preferred_element_type=jnp.float32),
        "head",
        scatter_dimension=0,
        tiled=True,
    )
    layer_out = summed.astype(jnp.bfloat16)
    groups = lax.axis_size("ctx")
    is_last = jnp.where(lax.axis_index("ctx") == groups - 1, 1.0, 0.0).astype(jnp.float32)
    own_columns = lax.psum_scatter(
        final_state.reshape(heads_here, DK * DV) * is_last, "ctx", scatter_dimension=1, tiled=True
    )
    every_head = lax.all_gather(own_columns, "head", axis=0, tiled=True)
    order_here = lax.dynamic_slice_in_dim(
        head_order, lax.axis_index("head") * heads_here, heads_here, 0
    )
    selector = (
        order_here[:, None] == jnp.arange(every_head.shape[0], dtype=jnp.int32)[None, :]
    ).astype(jnp.float32)
    decode_states = product("jh,hw->jw", selector, every_head)
    return (layer_out, decode_states)


def solution(mesh):
    in_specs = (
        P("ctx", "head"),
        P("ctx", "head"),
        P("ctx", "head"),
        P("ctx", "head"),
        P("ctx", "head"),
        P("ctx", "head"),
        P("ctx"),
        P(),
        P("head", None),
    )
    out_specs = (P(("ctx", "head"), None), P("head", "ctx"))
    return jax.shard_map(
        per_device, mesh=mesh, in_specs=in_specs, out_specs=out_specs, check_vma=False
    )
```

profile of v0, /device:TPU:13, one launch (start us, length us, event | category | flops | bytes accessed | tf_op | source)
XLA Modules:
  0.0 325.5 jit_solution(7972824543331888044)
XLA Ops:
  7.3 1.0 reshape.134
  8.8 0.8 reshape.128
  9.5 0.7 eq.84
  11.0 0.8 reshape.131
  12.5 1.0 fusion.23
  14.7 0.7 fusion.39
  16.1 0.7 fusion.37
  17.4 0.7 fusion.35
  18.7 0.7 fusion.33
  19.5 1.4 pad_add_fusion
  21.6 0.7 fusion.29
  22.4 0.7 fusion.31
  23.2 3.0 fusion.45
  26.2 2.2 convolution_subtract_fusion
  28.5 5.1 %while.33 = (s32[]{:T(128)}, f32[8,128,128]{2,1,0:T(8,128)S(1)}, f32[8,128,128]{2,1,0:T(8,128)S(1)}, f32[2,8,128,128]{3,2,1,0:T(8,128)}, f32[2,8,128,128]{3,2,1,...) while((s32[]{:T(128)}, f32[8,128,128]{2,1,0:T(8,128)S(1)}, ...), condition=%wide.region_4.5_spmd.clone, body=%wide.region_3.4_spmd.clone.sunk | while | flops 403046400 | bytes 12060307 | solution.py:138
  28.6 1.1 bitcast_dynamic-update-slice_fusion.5
  30.4 0.6 convolution_add_fusion.6
  31.1 1.1 bitcast_dynamic-update-slice_fusion.5
  32.9 0.6 convolution_add_fusion.6
  33.6 0.8 copy-done
  37.0 0.7 bitcast_dynamic-update-slice_fusion.3
  37.7 0.7 bitcast_dynamic-update-slice_fusion.2
  38.4 12.4 %all-reduce.2 = (f32[8]{0:T(128)S(1)}, f32[8]{0:T(128)S(1)}) all-reduce(f32[8]{0:T(128)S(1)} %bitcast_dynamic-update-slice_fusion.3, f32[8]{0:T(128)S(1)} %bitcast_dynamic-update-slice_fusion.2), channel_id=2, replica_groups=mesh['ctx'=8,'head'=4] {'ctx'}, use_global_device_ids=true, to_apply=%add | all-reduce | flops 16 | bytes 128 | tf_op jit(solution)/shard_map/all_gather | solution.py:17
  50.8 1.0 reshape.133
  52.4 1.0 convolution_multiply_fusion.2
  54.0 0.7 convolution_subtract_fusion.1
  54.7 1.1 convolution_add_fusion.2
  55.8 50.9 %all-gather.7.cloned.1.call-done = f32[64,128,128]{2,1,0:T(8,128)} async-done(((f32[8,128,128]{2,1,0:T(8,128)}), f32[64,128,128]{2,1,0:T(8,128)}) %all-gather.7.cloned.1.call-update) | async-done | bytes 4194320 | tf_op jit(solution)/shard_map/all_gather | solution.py:17
  106.7 73.8 %all-gather.9.cloned.1.call-done = f32[64,128,128]{2,1,0:T(8,128)} async-done(((f32[8,128,128]{2,1,0:T(8,128)}), f32[64,128,128]{2,1,0:T(8,128)}) %all-gather.9.cloned.1.call-update) | async-done | bytes 4194320 | tf_op jit(solution)/shard_map/all_gather | solution.py:17
  180.5 45.6 %while.34 = (s32[]{:T(128)}, f32[8,128,128]{2,1,0:T(8,128)S(1)}, f32[]{:T(128)}, s32[]{:T(128)}, f32[8]{0:T(128)S(1)}, /*index=5*/f32[8,8,128,128]{3,2,1,0:T(8,1...) while((s32[]{:T(128)}, f32[8,128,128]{2,1,0:T(8,128)S(1)}, ...), condition=%wide.region_6.7_spmd.clone, body=%wide.region_5.6_spmd.clone.sunk | while | flops 201981968 | bytes 3673336 | solution.py:27
  182.4 1.9 fusion.125
  188.1 1.9 fusion.125
  193.8 1.9 fusion.125
  199.5 1.9 fusion.125
  205.2 1.9 fusion.125
  210.9 1.9 fusion.125
  216.6 1.9 fusion.125
  222.3 1.9 fusion.125
  226.1 0.7 fusion.22
  226.8 1.1 copy.65
  228.2 2.3 convolution_bitcast_fusion
  230.5 2.2 multiply_reduce_fusion
  233.4 4.0 %fusion.48 = f32[128,2048]{1,0:T(8,128)} fusion(bf16[1024,2048]{1,0:T(8,128)(2,1)} %param.21, bf16[128,1024]{1,0:T(8,128)(2,1)S(1)} %copy-done.11, f32[16,8,8,128]{3,2,1,0:T(8,128)S(1)} %bitcast.147, f32[16,8,8,128]{3,2,1,0:T(8,128)S(1)} %bitcast.148), kind=kOutput, calls=%fused_computation.69 | convolution fusion | flops 537919488 | bytes 6553600 | tf_op jit(solution)/shard_map/dot_general | solution.py:156
  237.5 51.3 %reduce-scatter.5.cloned.1.call-done = f32[8,2048]{1,0:T(8,128)} async-done(((f32[8,16384]{1,0:T(8,128)}), f32[8,2048]{1,0:T(8,128)}) %reduce-scatter.5.cloned.1.call-update) | async-done | bytes 65552 | tf_op jit(solution)/shard_map/reduce_scatter | solution.py:164
  288.8 8.4 %all_gather.35 = f32[32,2048]{1,0:T(8,128)S(1)} all-gather(f32[8,2048]{1,0:T(8,128)} %reduce-scatter.5.cloned.1.call-done), channel_id=1, replica_groups=mesh['ctx'=8,'head'=4] {'head'}, dimensions={0}, use_global_device_ids=true | all-gather | bytes 327680 | tf_op jit(solution)/shard_map/all_gather | solution.py:167
  297.3 0.9 fusion.63
  298.1 19.2 %reduce-scatter.3.cloned.1.call-done = f32[32,2048]{1,0:T(8,128)} async-done(((f32[128,2048]{1,0:T(8,128)}), f32[32,2048]{1,0:T(8,128)}) %reduce-scatter.3.cloned.1.call-update) | async-done | bytes 262160 | tf_op jit(solution)/shard_map/reduce_scatter | solution.py:155
  317.3 1.6 convert_element_type.77
  (113 shorter events, 21.1 us)
Async XLA Ops:
  7.2 99.5 %all-gather.7.cloned.1.call-start = ((), (), s32[]{:S(2)}) async-start(), calls=%async_computation.4 | async-start | bytes 4718592 | tf_op jit(solution)/shard_map/all_gather | solution.py:17
  16.1 3.3 %copy-start.10 = (bf16[128,1024]{1,0:T(8,128)(2,1)S(1)}, bf16[128,1024]{1,0:T(8,128)(2,1)}, u32[]{:S(2)}) copy-start(bf16[128,1024]{1,0:T(8,128)(2,1)} %param.15) | copy-start | bytes 786436
  22.3 3.8 %copy-start.5 = (f32[2,8,64,128]{3,2,1,0:T(8,128)}, f32[2,8,64,128]{3,2,1,0:T(8,128)S(1)}, u32[]{:S(2)}) copy-start(f32[2,8,64,128]{3,2,1,0:T(8,128)S(1)} %fusion.29) | copy-start | bytes 1572868
  23.1 5.4 %copy-start.7 = (f32[2,8,64,128]{3,2,1,0:T(8,128)}, f32[2,8,64,128]{3,2,1,0:T(8,128)S(1)}, u32[]{:S(2)}) copy-start(f32[2,8,64,128]{3,2,1,0:T(8,128)S(1)} %fusion.31) | copy-start | bytes 1572868
  28.4 8.0 %copy-start.13 = (u32[32]{0:T(128)S(1)}, u32[32]{0:T(128)}, u32[]{:S(2)}) copy-start(u32[32]{0:T(128)} %constant.86) | copy-start | bytes 388
  28.5 1.8 copy-start.4
  31.1 1.8 copy-start.4
  33.5 0.8 copy-start
  33.5 1.0 copy-start.2
  33.6 19.8 %copy-start.6 = (f32[2,8,64,128]{3,2,1,0:T(8,128)S(1)}, f32[2,8,64,128]{3,2,1,0:T(8,128)}, u32[]{:S(2)}) copy-start(f32[2,8,64,128]{3,2,1,0:T(8,128)} %copy-done.5) | copy-start | bytes 1572868
  33.6 20.4 %copy-start.8 = (f32[2,8,64,128]{3,2,1,0:T(8,128)S(1)}, f32[2,8,64,128]{3,2,1,0:T(8,128)}, u32[]{:S(2)}) copy-start(f32[2,8,64,128]{3,2,1,0:T(8,128)} %copy-done.7) | copy-start | bytes 1572868
  34.4 146.1 %all-gather.9.cloned.1.call-start = ((), (), s32[]{:S(2)}) async-start(), calls=%async_computation.5 | async-start | bytes 4718592 | tf_op jit(solution)/shard_map/all_gather | solution.py:17
  34.4 20.3 %copy-start.9 = (f32[2,8,128,128]{3,2,1,0:T(8,128)S(1)}, f32[2,8,128,128]{3,2,1,0:T(8,128)}, u32[]{:S(2)}) copy-start(f32[2,8,128,128]{3,2,1,0:T(8,128)} %get-tuple-element.182) | copy-start | bytes 3145732
  35.1 253.7 %reduce-scatter.5.cloned.1.call-start = ((), (), s32[]{:S(2)}) async-start(), calls=%async_computation.3 | async-start | bytes 589824 | tf_op jit(solution)/shard_map/reduce_scatter | solution.py:164
  180.5 45.6 %copy-start.1 = (f32[8,128,128]{2,1,0:T(8,128)S(1)}, f32[8,128,128]{2,1,0:T(8,128)}, u32[]{:S(2)}) copy-start(f32[8,128,128]{2,1,0:T(8,128)} %copy-done) | copy-start | bytes 1572868
  180.5 45.6 %copy-start.3 = (f32[8,128,128]{2,1,0:T(8,128)S(1)}, f32[8,128,128]{2,1,0:T(8,128)}, u32[]{:S(2)}) copy-start(f32[8,128,128]{2,1,0:T(8,128)} %copy-done.2) | copy-start | bytes 1572868
  226.8 6.6 %copy-start.11 = (bf16[128,1024]{1,0:T(8,128)(2,1)S(1)}, bf16[128,1024]{1,0:T(8,128)(2,1)}, u32[]{:S(2)}) copy-start(bf16[128,1024]{1,0:T(8,128)(2,1)} %param.16) | copy-start | bytes 786436
  227.9 89.4 %reduce-scatter.3.cloned.1.call-start = ((), (), s32[]{:S(2)}) async-start(), calls=%async_computation.2 | async-start | bytes 1310720 | tf_op jit(solution)/shard_map/reduce_scatter | solution.py:155
  233.2 4.3 %copy-start.12 = (s32[32]{0:T(128)S(1)}, s32[32]{0:T(128)}, u32[]{:S(2)}) copy-start(s32[32]{0:T(128)} %param.20) | copy-start | bytes 388
Sparse Core Ops, SparseCore 0:
  34.5 72.1 all-gather.6
  108.8 71.6 all-gather.8
  228.1 60.7 reduce-scatter.4
  291.4 25.9 reduce-scatter.2
where the time goes:
time: 328 us; the launch traced here: 326 us
  waiting for transfers between devices  196 us (60%)
  matrix products  45.1 us (14%)
  blocking collectives  20.9 us (6%)
  loops' own time  20.7 us (6%)
  local copies, waits for them, and re-layouts  20 us (6%)
  between operations  15.6 us (5%)
  other arithmetic  6.93 us (2%)
    all_gather x2, waiting for transfers between devices, prefix(): everything = jax.tree.map(lambda part: lax.all_gather(part, axis), x)  125 us
    reduce_scatter x1, waiting for transfers between devices, per_device(): lax.psum_scatter(final_state.reshape(heads_here, DK * DV) * is_last, 'ctx...  51.3 us
    dot_general x35, matrix products, product(): return jnp.einsum(form, left, right, precision=highest)  41 us
    another operation x1, loops' own time, prefix(): return lax.fori_loop(0, peers, step, start)  20.6 us
    reduce_scatter x1, waiting for transfers between devices, per_device(): lax.psum_scatter(jnp.dot(normed, out_weight, preferred_element_type=jnp.f...  19.2 us
    all_gather x1, blocking collectives, prefix(): everything = jax.tree.map(lambda part: lax.all_gather(part, axis), x)  12.4 us
    dynamic_slice x16, local copies, waits for them, and re-layouts, step(): new = combine(before, jax.tree.map(lambda part: part[k], everything))  9.63 us
    all_gather x1, blocking collectives, per_device(): every_head = lax.all_gather(own_columns, 'head', axis=0, tiled=True)  8.43 us
  transfers between devices with their start and end apart: 4, of which 4 were waited for; matrix products, arithmetic and copies ran while one was open for 5% of the time, Pallas kernels for 0%

commit v1 on v0

--- a/solution.py
+++ b/solution.py
@@ -1,6 +1,10 @@
+import functools
+
 import jax
 import jax.numpy as jnp
 from jax import lax
+from jax.experimental import pallas as pl
+from jax.experimental.pallas import tpu as pltpu
 from jax.sharding import PartitionSpec as P
 
 DK = 128
@@ -98,7 +102,7 @@
     return (through, reached, first_doc, last_doc)
 
 
-def per_device(
+def gathered_prefix(
     queries, keys, values, out_gate, log_decay, write_strength, segment_ids, head_order, out_weight
 ):
     tok_rows = queries.shape[0]
@@ -175,6 +179,417 @@
     return (layer_out, decode_states)
 
 
+MESH = pl.DeviceIdType.MESH
+COLUMN_TILE = 512
+META_ROWS = 16
+
+
+def mxu(left, right):
+    return jnp.dot(
+        left.astype(jnp.bfloat16), right.astype(jnp.bfloat16), preferred_element_type=jnp.float32
+    )
+
+
+def inverse_by_halves(coupling, row_at, col_at):
+    size = coupling.shape[0]
+    eye = (row_at == col_at).astype(jnp.float32)
+    inverse = eye - jnp.where(row_at // 2 == col_at // 2, coupling, 0.0)
+    half = 2
+    while half < size:
+        within = (row_at // (2 * half) == col_at // (2 * half)) & (row_at // half != col_at // half)
+        below = jnp.where(within, coupling, 0.0)
+        inverse = inverse - mxu(mxu(inverse, below), inverse)
+        half *= 2
+    return inverse
+
+
+def layer_kernel(
+    ctx_size,
+    head_size,
+    q_ref,
+    k_ref,
+    v_ref,
+    gate_ref,
+    decay_ref,
+    strength_ref,
+    doc_ref,
+    order_ref,
+    weight_ref,
+    out_ref,
+    decode_ref,
+    weight,
+    decay_cols,
+    strength_cols,
+    decay_rows,
+    outbox,
+    inbox,
+    entering,
+    arrived,
+    local,
+    reader,
+    normed,
+    final,
+    columns,
+    partial,
+    leaving,
+    summands,
+    weight_sem,
+    map_send,
+    map_recv,
+    state_send,
+    state_recv,
+    final_send,
+    final_recv,
+    column_send,
+    column_recv,
+    sum_send,
+    sum_recv,
+):
+    me = lax.axis_index("ctx")
+    group = lax.axis_index("head")
+    rows = q_ref.shape[0]
+    key_groups = q_ref.shape[1] // DK
+    heads = v_ref.shape[1] // DV
+    share = heads // key_groups
+    own_rows = rows // head_size
+    state_rows = DK // ctx_size
+    width = weight.shape[1]
+    tiles = width // COLUMN_TILE
+
+    barrier = pltpu.get_barrier_semaphore()
+    for away in range(1, ctx_size):
+        pl.semaphore_signal(
+            barrier, inc=1, device_id=(lax.rem(me + away, ctx_size), group), device_id_type=MESH
+        )
+    for away in range(1, head_size):
+        pl.semaphore_signal(
+            barrier, inc=1, device_id=(me, lax.rem(group + away, head_size)), device_id_type=MESH
+        )
+    fetch = pltpu.make_async_copy(weight_ref, weight, weight_sem)
+    fetch.start()
+
+    row_at = lax.broadcasted_iota(jnp.int32, (rows, rows), 0)
+    col_at = lax.broadcasted_iota(jnp.int32, (rows, rows), 1)
+    causal = row_at >= col_at
+    strict = row_at > col_at
+    eye = (row_at == col_at).astype(jnp.float32)
+    cumulative = jnp.dot(
+        causal.astype(jnp.float32),
+        decay_ref[...],
+        precision=highest,
+        preferred_element_type=jnp.float32,
+    )
+    for h in range(heads):
+        spread = jnp.broadcast_to(cumulative[:, h : h + 1], (rows, rows))
+        decay_cols[h] = spread
+        decay_rows[h] = spread.T[0:8]
+        strength_cols[h] = jnp.broadcast_to(strength_ref[:, h : h + 1], (rows, rows))
+    doc_row = doc_ref[...].astype(jnp.float32)
+    doc_cols = jnp.broadcast_to(doc_row, (rows, rows)).T
+    same_doc = (doc_cols == doc_row) & causal
+    first_doc = doc_cols[0:1]
+    last_doc = doc_cols[rows - 1 : rows]
+    continues = doc_cols == first_doc
+    meta_at = lax.broadcasted_iota(jnp.int32, (META_ROWS, rows), 0)
+
+    pl.semaphore_wait(barrier, ctx_size - 1 + head_size - 1)
+
+    def map_copy(h):
+        return pltpu.make_async_remote_copy(
+            src_ref=outbox.at[h],
+            dst_ref=inbox.at[me],
+            send_sem=map_send.at[h],
+            recv_sem=map_recv.at[me],
+            device_id=(h, group),
+            device_id_type=MESH,
+        )
+
+    def key_group(turn, _):
+        kh = lax.rem(me // share + 1 + turn, key_groups)
+        at = pl.ds(pl.multiple_of(kh * DK, DK), DK)
+        query_raw = q_ref[:, at]
+        key_raw = k_ref[:, at]
+        query_wide = query_raw.astype(jnp.float32)
+        key_wide = key_raw.astype(jnp.float32)
+        query_scale = lax.rsqrt(
+            jnp.sum(query_wide * query_wide, axis=-1, keepdims=True) + norm_eps
+        ) * DK ** (-0.5)
+        key_scale = lax.rsqrt(jnp.sum(key_wide * key_wide, axis=-1, keepdims=True) + norm_eps)
+        query_part = query_wide * query_scale
+        key_part = key_wide * key_scale
+        key_across = key_part.T
+        key_scale_row = jnp.broadcast_to(key_scale, (rows, rows)).T
+        raw_across = key_wide.T
+        key_overlap = mxu(key_raw, raw_across) * key_scale * key_scale_row
+        query_overlap = mxu(query_raw, raw_across) * query_scale * key_scale_row
+        for member in range(share):
+            h = kh * share + member
+            decay = decay_cols[h]
+            strength = strength_cols[h]
+            mixing = jnp.where(
+                same_doc, jnp.exp(jnp.minimum(decay - decay_rows[h][0:1], 0.0)), 0.0
+            )
+            entry = jnp.where(continues, jnp.exp(decay), 0.0)
+            coupling = jnp.where(strict, strength * mixing * key_overlap, 0.0)
+            inverse = inverse_by_halves(coupling, row_at, col_at)
+            value_at = pl.ds(pl.multiple_of(h * DV, DV), DV)
+            value_part = v_ref[:, value_at].astype(jnp.float32)
+            sides = jnp.concatenate(
+                [strength * entry * key_part, strength * value_part], axis=1
+            )
+            sides = sides + mxu(inverse - eye, sides)
+            seen = mxu(mixing * query_overlap, sides)
+            local[h] = seen[:, DK:]
+            reader[h] = (entry * query_part - seen[:, :DK]).astype(jnp.bfloat16)
+            moved = mxu(key_across * mixing[rows - 1 : rows], sides)
+            outbox[h, 0:DK, :] = (-moved[:, :DK]).astype(jnp.bfloat16)
+            outbox[h, DK : 2 * DK, :] = moved[:, DK:].astype(jnp.bfloat16)
+            kept = entry[rows - 1 : rows]
+            kept_high = kept.astype(jnp.bfloat16).astype(jnp.float32)
+            meta = jnp.where(
+                meta_at == 0,
+                kept_high,
+                jnp.where(
+                    meta_at == 1, kept - kept_high, jnp.where(meta_at == 2, first_doc, last_doc)
+                ),
+            )
+            outbox[h, 2 * DK : 2 * DK + META_ROWS, :] = meta.astype(jnp.bfloat16)
+        for member in range(share):
+            h = kh * share + member
+
+            @pl.when(h != me)
+            def _():
+                map_copy(h).start()
+
+            @pl.when(h == me)
+            def _():
+                inbox[me] = outbox[me]
+
+        return 0
+
+    lax.fori_loop(0, key_groups, key_group, 0)
+
+    def state_copy(i):
+        return pltpu.make_async_remote_copy(
+            src_ref=entering.at[i],
+            dst_ref=arrived.at[me],
+            send_sem=state_send.at[i],
+            recv_sem=state_recv.at[me],
+            device_id=(i, group),
+            device_id_type=MESH,
+        )
+
+    def landed(buffer, slot, send, recv):
+        return pltpu.make_async_remote_copy(
+            src_ref=buffer.at[slot],
+            dst_ref=buffer.at[slot],
+            send_sem=send.at[slot],
+            recv_sem=recv.at[slot],
+            device_id=(slot, group),
+            device_id_type=MESH,
+        )
+
+    state = jnp.zeros((DK, DV), jnp.float32)
+    doc_before = None
+    for i in range(ctx_size):
+
+        @pl.when(me != i)
+        def _():
+            landed(inbox, i, map_send, map_recv).wait_recv()
+
+        meta = inbox[i, 2 * DK : 2 * DK + META_ROWS, :].astype(jnp.float32)
+        if i > 0:
+            state = jnp.where(meta[2:3] == doc_before, state, 0.0)
+        doc_before = meta[3:4]
+        state_low = state.astype(jnp.bfloat16)
+        entering[i] = state_low
+
+        @pl.when(me != i)
+        def _():
+            state_copy(i).start()
+
+        @pl.when(me == i)
+        def _():
+            arrived[i] = entering[i]
+
+        added = inbox[i, DK : 2 * DK, :].astype(jnp.float32)
+        state = (meta[0:1] + meta[1:2]) * state + mxu(inbox[i, 0:DK, :], state_low) + added
+    final[...] = state
+
+    head_here = group * heads + me
+
+    def final_copy(c):
+        return pltpu.make_async_remote_copy(
+            src_ref=final.at[pl.ds(pl.multiple_of(c * state_rows, state_rows), state_rows)],
+            dst_ref=columns.at[head_here],
+            send_sem=final_send.at[c],
+            recv_sem=final_recv.at[me],
+            device_id=(c, group),
+            device_id_type=MESH,
+        )
+
+    for away in range(1, ctx_size):
+        final_copy(lax.rem(me + away, ctx_size)).start()
+    columns[head_here] = final[pl.ds(pl.multiple_of(me * state_rows, state_rows), state_rows)]
+
+    for h in range(heads):
+
+        @pl.when(me != h)
+        def _():
+            landed(arrived, h, state_send, state_recv).wait_recv()
+
+        attention = local[h] + mxu(reader[h], arrived[h])
+        mean_square = jnp.mean(attention * attention, axis=-1, keepdims=True)
+        gate = gate_ref[:, h * DV : (h + 1) * DV].astype(jnp.float32)
+        gated = attention * lax.rsqrt(mean_square + norm_eps) * (gate / (1.0 + jnp.exp(-gate)))
+        normed[:, h * DV : (h + 1) * DV] = gated.astype(jnp.bfloat16)
+
+    fetch.wait()
+
+    def sum_copy(tile, away):
+        peer = lax.rem(group + away, head_size)
+        return pltpu.make_async_remote_copy(
+            src_ref=leaving.at[tile, pl.ds(pl.multiple_of(peer * own_rows, own_rows), own_rows)],
+            dst_ref=summands.at[tile, away],
+            send_sem=sum_send.at[tile, away],
+            recv_sem=sum_recv.at[tile, away],
+            device_id=(me, peer),
+            device_id_type=MESH,
+        )
+
+    for tile in range(tiles):
+        at = slice(tile * COLUMN_TILE, (tile + 1) * COLUMN_TILE)
+        product_here = jnp.dot(normed[...], weight[:, at], preferred_element_type=jnp.float32)
+        partial[:, at] = product_here
+        leaving[tile] = product_here.astype(jnp.bfloat16)
+        for away in range(1, head_size):
+            sum_copy(tile, away).start()
+
+    for away in range(1, ctx_size):
+        source = lax.rem(me + away, ctx_size)
+        pltpu.make_async_remote_copy(
+            src_ref=columns.at[group * heads + source],
+            dst_ref=columns.at[group * heads + source],
+            send_sem=final_send.at[source],
+            recv_sem=final_recv.at[source],
+            device_id=(source, group),
+            device_id_type=MESH,
+        ).wait_recv()
+
+    def column_copy(peer, block, slot):
+        return pltpu.make_async_remote_copy(
+            src_ref=columns.at[pl.ds(block * heads, heads)],
+            dst_ref=columns.at[pl.ds(block * heads, heads)],
+            send_sem=column_send.at[slot],
+            recv_sem=column_recv.at[slot],
+            device_id=(me, peer),
+            device_id_type=MESH,
+        )
+
+    for away in range(1, head_size):
+        column_copy(lax.rem(group + away, head_size), group, away).start()
+
+    for tile in range(tiles):
+        at = slice(tile * COLUMN_TILE, (tile + 1) * COLUMN_TILE)
+        total = partial[pl.ds(pl.multiple_of(group * own_rows, own_rows), own_rows), at]
+        for away in range(1, head_size):
+            sum_copy(tile, away).wait_recv()
+            total = total + summands[tile, away].astype(jnp.float32)
+        out_ref[:, at] = total.astype(jnp.bfloat16)
+
+    for away in range(1, head_size):
+        source = lax.rem(group + head_size - away, head_size)
+        column_copy(source, source, away).wait_recv()
+    for slot in range(heads):
+        chosen = columns[order_ref[group * heads + slot]]
+        for r in range(state_rows):
+            decode_ref[slot : slot + 1, r * DV : (r + 1) * DV] = chosen[r : r + 1]
+
+    for away in range(1, ctx_size):
+        other = lax.rem(me + away, ctx_size)
+        map_copy(other).wait_send()
+        state_copy(other).wait_send()
+        final_copy(other).wait_send()
+    for away in range(1, head_size):
+        column_copy(lax.rem(group + away, head_size), group, away).wait_send()
+        for tile in range(tiles):
+            sum_copy(tile, away).wait_send()
+
+
+def head_owner(
+    queries, keys, values, out_gate, log_decay, write_strength, segment_ids, head_order, out_weight
+):
+    rows = queries.shape[0]
+    heads = values.shape[1] // DV
+    ctx_size, head_size = lax.axis_size("ctx"), lax.axis_size("head")
+    width = out_weight.shape[1]
+    tiles = width // COLUMN_TILE
+    own_rows = rows // head_size
+    state_rows = DK // ctx_size
+    f32, bf16 = jnp.float32, jnp.bfloat16
+    dma = pltpu.SemaphoreType.DMA
+    vmem = pl.BlockSpec(memory_space=pltpu.VMEM)
+    return pl.pallas_call(
+        functools.partial(layer_kernel, ctx_size, head_size),
+        out_shape=(
+            jax.ShapeDtypeStruct((own_rows, width), bf16),
+            jax.ShapeDtypeStruct((heads, state_rows * DV), f32),
+        ),
+        in_specs=[vmem] * 7
+        + [pl.BlockSpec(memory_space=pltpu.SMEM), pl.BlockSpec(memory_space=pl.ANY)],
+        out_specs=(vmem, vmem),
+        scratch_shapes=[
+            pltpu.VMEM(out_weight.shape, bf16),
+            pltpu.VMEM((heads, rows, rows), f32),
+            pltpu.VMEM((heads, rows, rows), f32),
+            pltpu.VMEM((heads, 8, rows), f32),
+            pltpu.VMEM((heads, 2 * DK + META_ROWS, DV), bf16),
+            pltpu.VMEM((ctx_size, 2 * DK + META_ROWS, DV), bf16),
+            pltpu.VMEM((ctx_size, DK, DV), bf16),
+            pltpu.VMEM((heads, DK, DV), bf16),
+            pltpu.VMEM((heads, rows, DV), f32),
+            pltpu.VMEM((heads, rows, DK), bf16),
+            pltpu.VMEM((rows, heads * DV), bf16),
+            pltpu.VMEM((DK, DV), f32),
+            pltpu.VMEM((head_size * heads, state_rows, DV), f32),
+            pltpu.VMEM((rows, width), f32),
+            pltpu.VMEM((tiles, rows, COLUMN_TILE), bf16),
+            pltpu.VMEM((tiles, head_size, own_rows, COLUMN_TILE), bf16),
+            dma,
+            dma((heads,)),
+            dma((ctx_size,)),
+            dma((ctx_size,)),
+            dma((heads,)),
+            dma((ctx_size,)),
+            dma((ctx_size,)),
+            dma((head_size,)),
+            dma((head_size,)),
+            dma((tiles, head_size)),
+            dma((tiles, head_size)),
+        ],
+        compiler_params=pltpu.CompilerParams(
+            collective_id=0, has_side_effects=True, vmem_limit_bytes=40 * 1024 * 1024
+        ),
+    )(
+        queries,
+        keys,
+        values,
+        out_gate,
+        log_decay,
+        write_strength,
+        segment_ids.reshape(1, rows),
+        head_order,
+        out_weight,
+    )
+
+
+def per_device(queries, keys, values, *rest):
+    heads = values.shape[1] // DV
+    one_owner_per_head = heads == lax.axis_size("ctx") and queries.shape[0] == DK
+    form = head_owner if one_owner_per_head else gathered_prefix
+    return form(queries, keys, values, *rest)
+
+
 def solution(mesh):
     in_specs = (
         P("ctx", "head"),

time: 328 us -> 52.6 us (0.16)
  the two profiles are of different devices: /device:TPU:13 before, /device:TPU:31 now
where the time goes in v1:
time: 52.6 us; the launch traced here: 52.3 us
  Pallas kernels  41.6 us (79%)
  local copies, waits for them, and re-layouts  10.1 us (19%)
  between operations  0.65 us (1%)
    pallas_call x1, Pallas kernels, head_owner(): pl.pallas_call(functools.partial(layer_kernel, ctx_size, head_size), out_...  41.6 us
    unnamed x18, local copies, waits for them, and re-layouts  10.1 us

profile of v1, /device:TPU:31, one launch (start us, length us, event | category | flops | bytes accessed | tf_op | source)
XLA Modules:
  0.0 52.3 jit_solution(195345045627898792)
XLA Ops:
  0.6 0.8 %copy.11.decay_ref = f32[128,8]{1,0:T(8,128)S(1)} copy(f32[128,8]{0,1:T(8,128)} %param.13) | data formatting | bytes 8192 | tf_op args[4]
  1.4 0.8 %copy.12.strength_ref = f32[128,8]{1,0:T(8,128)S(1)} copy(f32[128,8]{0,1:T(8,128)} %param.14) | data formatting | bytes 8192 | tf_op args[5]
  2.2 0.0 copy-start
  2.2 2.2 %copy-done = bf16[1024,2048]{1,0:T(8,128)(2,1)S(1)} copy-done((bf16[1024,2048]{1,0:T(8,128)(2,1)S(1)}, bf16[1024,2048]{1,0:T(8,128)(2,1)}, u32[]{:S(2)}) %copy-start) | copy-done | bytes 4194328
  4.4 0.0 copy-start.1
  4.4 0.9 %copy-done.1 = bf16[128,1024]{1,0:T(8,128)(2,1)S(1)} copy-done((bf16[128,1024]{1,0:T(8,128)(2,1)S(1)}, bf16[128,1024]{1,0:T(8,128)(2,1)}, u32[]{:S(2)}) %copy-start.1) | copy-done | bytes 262168
  5.3 0.0 copy-start.2
  5.3 0.9 %copy-done.2 = bf16[128,1024]{1,0:T(8,128)(2,1)S(1)} copy-done((bf16[128,1024]{1,0:T(8,128)(2,1)S(1)}, bf16[128,1024]{1,0:T(8,128)(2,1)}, u32[]{:S(2)}) %copy-start.2) | copy-done | bytes 262168
  6.3 0.0 copy-start.3
  6.3 0.9 %copy-done.3 = bf16[128,512]{1,0:T(8,128)(2,1)S(1)} copy-done((bf16[128,512]{1,0:T(8,128)(2,1)S(1)}, bf16[128,512]{1,0:T(8,128)(2,1)}, u32[]{:S(2)}) %copy-start.3) | copy-done | bytes 131096
  7.2 0.0 copy-start.4
  7.2 0.9 %copy-done.4 = bf16[128,512]{1,0:T(8,128)(2,1)S(1)} copy-done((bf16[128,512]{1,0:T(8,128)(2,1)S(1)}, bf16[128,512]{1,0:T(8,128)(2,1)}, u32[]{:S(2)}) %copy-start.4) | copy-done | bytes 131096
  8.1 0.0 copy-start.5
  8.1 0.7 %copy-done.5 = s32[128]{0:T(128)S(1)} copy-done((s32[128]{0:T(128)S(1)}, s32[128]{0:T(128)}, u32[]{:S(2)}) %copy-start.5) | copy-done | bytes 536
  8.8 0.0 copy-start.6
  8.8 0.7 %copy-done.6 = s32[32]{0:T(128)S(1)} copy-done((s32[32]{0:T(128)S(1)}, s32[32]{0:T(128)}, u32[]{:S(2)}) %copy-start.6) | copy-done | bytes 152
  9.4 41.6 %shard_map.104 = (bf16[32,2048]{1,0:T(8,128)(2,1)S(1)}, f32[8,2048]{1,0:T(8,128)S(1)}) custom-call(bf16[128,512]{1,0:T(8,128)(2,1)S(1)} %copy-done.3, bf16[128,512]{1,0:T(8,128)(2,1)S(1)} %copy-done.4, bf16[128,1024]{1,0:T(8,128)(2,1)S(1)} %copy-done.1, bf16[128,1024]{1,0:T(8,128)(2,1)S(1)} %copy-done.2, f32[128,8]{1,0:T(8,128)S(1)} %copy.11.decay_ref, ...), custom_call_target="tpu_custom_call" | custom-call | tf_op jit(solution)/shard_map/pallas_call | solution.py:532
  51.0 0.7 %copy.15 = bf16[32,2048]{1,0:T(8,128)(2,1)} copy(bf16[32,2048]{1,0:T(8,128)(2,1)S(1)} %get-tuple-element.4) | data formatting | bytes 262144
  51.7 0.6 %copy.16 = f32[8,2048]{1,0:T(8,128)} copy(f32[8,2048]{1,0:T(8,128)S(1)} %get-tuple-element.5) | data formatting | bytes 131072
Async XLA Ops:
  2.2 2.2 %copy-start = (bf16[1024,2048]{1,0:T(8,128)(2,1)S(1)}, bf16[1024,2048]{1,0:T(8,128)(2,1)}, u32[]{:S(2)}) copy-start(bf16[1024,2048]{1,0:T(8,128)(2,1)} %weight_ref.1) | copy-start | bytes 12582916
  4.4 0.9 %copy-start.1 = (bf16[128,1024]{1,0:T(8,128)(2,1)S(1)}, bf16[128,1024]{1,0:T(8,128)(2,1)}, u32[]{:S(2)}) copy-start(bf16[128,1024]{1,0:T(8,128)(2,1)} %v_ref.1) | copy-start | bytes 786436
  5.3 0.9 %copy-start.2 = (bf16[128,1024]{1,0:T(8,128)(2,1)S(1)}, bf16[128,1024]{1,0:T(8,128)(2,1)}, u32[]{:S(2)}) copy-start(bf16[128,1024]{1,0:T(8,128)(2,1)} %gate_ref.1) | copy-start | bytes 786436
  6.3 0.9 %copy-start.3 = (bf16[128,512]{1,0:T(8,128)(2,1)S(1)}, bf16[128,512]{1,0:T(8,128)(2,1)}, u32[]{:S(2)}) copy-start(bf16[128,512]{1,0:T(8,128)(2,1)} %q_ref.1) | copy-start | bytes 393220
  7.2 0.9 %copy-start.4 = (bf16[128,512]{1,0:T(8,128)(2,1)S(1)}, bf16[128,512]{1,0:T(8,128)(2,1)}, u32[]{:S(2)}) copy-start(bf16[128,512]{1,0:T(8,128)(2,1)} %k_ref.1) | copy-start | bytes 393220
  8.1 0.7 %copy-start.5 = (s32[128]{0:T(128)S(1)}, s32[128]{0:T(128)}, u32[]{:S(2)}) copy-start(s32[128]{0:T(128)} %param.15) | copy-start | bytes 1540
  8.8 0.7 %copy-start.6 = (s32[32]{0:T(128)S(1)}, s32[32]{0:T(128)}, u32[]{:S(2)}) copy-start(s32[32]{0:T(128)} %order_ref.1) | copy-start | bytes 388

commit v2 on v1

--- a/solution.py
+++ b/solution.py
@@ -190,22 +190,56 @@
     )
 
 
-def inverse_by_halves(coupling, row_at, col_at):
-    size = coupling.shape[0]
+def split(wide):
+    high = wide.astype(jnp.bfloat16)
+    return high, (wide - high.astype(jnp.float32)).astype(jnp.bfloat16)
+
+
+def mxu_wide_left(left, right):
+    high, low = split(left)
+    right = right.astype(jnp.bfloat16)
+    return mxu(jnp.concatenate([high, low], axis=1), jnp.concatenate([right, right], axis=0))
+
+
+def mxu_wide(left, right):
+    left_high, left_low = split(left)
+    right_high, right_low = split(right)
+    return mxu(
+        jnp.concatenate([left_high, left_low, left_high], axis=1),
+        jnp.concatenate([right_high, right_high, right_low], axis=0),
+    )
+
+
+def inverses_less_eye(couplings, row_at, col_at):
+    size = couplings[0].shape[0]
     eye = (row_at == col_at).astype(jnp.float32)
-    inverse = eye - jnp.where(row_at // 2 == col_at // 2, coupling, 0.0)
+    pairs = row_at // 2 == col_at // 2
+    found = [eye - jnp.where(pairs, coupling, 0.0) for coupling in couplings]
     half = 2
     while half < size:
         within = (row_at // (2 * half) == col_at // (2 * half)) & (row_at // half != col_at // half)
-        below = jnp.where(within, coupling, 0.0)
-        inverse = inverse - mxu(mxu(inverse, below), inverse)
+        below = [mxu(x, jnp.where(within, c, 0.0)) for x, c in zip(found, couplings)]
+        found = [x - mxu(b, x) for x, b in zip(found, below)]
         half *= 2
-    return inverse
+    found = [x - eye for x in found]
+    residue = [-x - c - mxu_wide(c, x) for x, c in zip(found, couplings)]
+    return [x + r + mxu(x, r) for x, r in zip(found, residue)]
 
 
 def layer_kernel(
     ctx_size,
     head_size,
+    q_hbm,
+    k_hbm,
+    v_hbm,
+    gate_hbm,
+    decay_hbm,
+    strength_hbm,
+    doc_hbm,
+    order_ref,
+    weight_ref,
+    out_ref,
+    decode_ref,
     q_ref,
     k_ref,
     v_ref,
@@ -213,11 +247,8 @@
     decay_ref,
     strength_ref,
     doc_ref,
-    order_ref,
-    weight_ref,
-    out_ref,
-    decode_ref,
     weight,
+    opened,
     decay_cols,
     strength_cols,
     decay_rows,
@@ -233,6 +264,7 @@
     partial,
     leaving,
     summands,
+    fetch_sem,
     weight_sem,
     map_send,
     map_recv,
@@ -265,25 +297,42 @@
         pl.semaphore_signal(
             barrier, inc=1, device_id=(me, lax.rem(group + away, head_size)), device_id_type=MESH
         )
-    fetch = pltpu.make_async_copy(weight_ref, weight, weight_sem)
-    fetch.start()
+    fetches = [
+        pltpu.make_async_copy(source, held, fetch_sem.at[slot])
+        for slot, (source, held) in enumerate(
+            (
+                (decay_hbm, decay_ref),
+                (strength_hbm, strength_ref),
+                (doc_hbm, doc_ref),
+                (q_hbm, q_ref),
+                (k_hbm, k_ref),
+                (v_hbm, v_ref),
+                (gate_hbm, gate_ref),
+            )
+        )
+    ]
+    for fetch in fetches:
+        fetch.start()
+    weight_fetch = pltpu.make_async_copy(weight_ref, weight, weight_sem)
+    weight_fetch.start()
 
     row_at = lax.broadcasted_iota(jnp.int32, (rows, rows), 0)
     col_at = lax.broadcasted_iota(jnp.int32, (rows, rows), 1)
     causal = row_at >= col_at
     strict = row_at > col_at
-    eye = (row_at == col_at).astype(jnp.float32)
+    for fetch in fetches[:3]:
+        fetch.wait()
     cumulative = jnp.dot(
-        causal.astype(jnp.float32),
         decay_ref[...],
+        (row_at <= col_at).astype(jnp.float32),
         precision=highest,
         preferred_element_type=jnp.float32,
     )
     for h in range(heads):
-        spread = jnp.broadcast_to(cumulative[:, h : h + 1], (rows, rows))
-        decay_cols[h] = spread
-        decay_rows[h] = spread.T[0:8]
-        strength_cols[h] = jnp.broadcast_to(strength_ref[:, h : h + 1], (rows, rows))
+        spread = jnp.broadcast_to(cumulative[h : h + 1], (rows, rows))
+        decay_cols[h] = spread.T
+        decay_rows[h] = spread[0:8]
+        strength_cols[h] = jnp.broadcast_to(strength_ref[h : h + 1, :], (rows, rows)).T
     doc_row = doc_ref[...].astype(jnp.float32)
     doc_cols = jnp.broadcast_to(doc_row, (rows, rows)).T
     same_doc = (doc_cols == doc_row) & causal
@@ -292,6 +341,8 @@
     continues = doc_cols == first_doc
     meta_at = lax.broadcasted_iota(jnp.int32, (META_ROWS, rows), 0)
 
+    for fetch in fetches[3:6]:
+        fetch.wait()
     pl.semaphore_wait(barrier, ctx_size - 1 + head_size - 1)
 
     def map_copy(h):
@@ -304,44 +355,54 @@
             device_id_type=MESH,
         )
 
-    def key_group(turn, _):
-        kh = lax.rem(me // share + 1 + turn, key_groups)
-        at = pl.ds(pl.multiple_of(kh * DK, DK), DK)
-        query_raw = q_ref[:, at]
-        key_raw = k_ref[:, at]
-        query_wide = query_raw.astype(jnp.float32)
-        key_wide = key_raw.astype(jnp.float32)
-        query_scale = lax.rsqrt(
-            jnp.sum(query_wide * query_wide, axis=-1, keepdims=True) + norm_eps
-        ) * DK ** (-0.5)
-        key_scale = lax.rsqrt(jnp.sum(key_wide * key_wide, axis=-1, keepdims=True) + norm_eps)
-        query_part = query_wide * query_scale
-        key_part = key_wide * key_scale
-        key_across = key_part.T
-        key_scale_row = jnp.broadcast_to(key_scale, (rows, rows)).T
-        raw_across = key_wide.T
-        key_overlap = mxu(key_raw, raw_across) * key_scale * key_scale_row
-        query_overlap = mxu(query_raw, raw_across) * query_scale * key_scale_row
-        for member in range(share):
-            h = kh * share + member
+    together = 2 if key_groups % 2 == 0 else 1
+
+    def some_heads(turn, _):
+        overlaps = []
+        for j in range(together):
+            kh = lax.rem(me // share + 1 + turn * together + j, key_groups)
+            at = pl.ds(pl.multiple_of(kh * DK, DK), DK)
+            query_raw = q_ref[:, at]
+            key_raw = k_ref[:, at]
+            query_wide = query_raw.astype(jnp.float32)
+            key_wide = key_raw.astype(jnp.float32)
+            query_scale = lax.rsqrt(
+                jnp.sum(query_wide * query_wide, axis=-1, keepdims=True) + norm_eps
+            ) * DK ** (-0.5)
+            key_scale = lax.rsqrt(jnp.sum(key_wide * key_wide, axis=-1, keepdims=True) + norm_eps)
+            key_scale_row = jnp.broadcast_to(key_scale, (rows, rows)).T
+            raw_across = key_wide.T
+            key_overlap = mxu(key_raw, raw_across) * key_scale * key_scale_row
+            query_overlap = mxu(query_raw, raw_across) * query_scale * key_scale_row
+            parts = (
+                query_wide * query_scale,
+                key_wide * key_scale,
+                raw_across * key_scale_row,
+                key_overlap,
+                query_overlap,
+            )
+            overlaps.extend((kh * share + member, parts) for member in range(share))
+        mixings, entries, couplings = [], [], []
+        for h, parts in overlaps:
             decay = decay_cols[h]
-            strength = strength_cols[h]
             mixing = jnp.where(
                 same_doc, jnp.exp(jnp.minimum(decay - decay_rows[h][0:1], 0.0)), 0.0
             )
-            entry = jnp.where(continues, jnp.exp(decay), 0.0)
-            coupling = jnp.where(strict, strength * mixing * key_overlap, 0.0)
-            inverse = inverse_by_halves(coupling, row_at, col_at)
+            mixings.append(mixing)
+            entries.append(jnp.where(continues, jnp.exp(decay), 0.0))
+            couplings.append(jnp.where(strict, strength_cols[h] * mixing * parts[3], 0.0))
+        solved = inverses_less_eye(couplings, row_at, col_at)
+        sides = []
+        for (h, parts), entry in zip(overlaps, entries):
             value_at = pl.ds(pl.multiple_of(h * DV, DV), DV)
+            strength = strength_cols[h]
             value_part = v_ref[:, value_at].astype(jnp.float32)
-            sides = jnp.concatenate(
-                [strength * entry * key_part, strength * value_part], axis=1
+            sides.append(
+                jnp.concatenate([strength * entry * parts[1], strength * value_part], axis=1)
             )
-            sides = sides + mxu(inverse - eye, sides)
-            seen = mxu(mixing * query_overlap, sides)
-            local[h] = seen[:, DK:]
-            reader[h] = (entry * query_part - seen[:, :DK]).astype(jnp.bfloat16)
-            moved = mxu(key_across * mixing[rows - 1 : rows], sides)
+        sides = [side + mxu_wide(x, side) for x, side in zip(solved, sides)]
+        for (h, parts), entry, mixing, side in zip(overlaps, entries, mixings, sides):
+            moved = mxu_wide(parts[2] * mixing[rows - 1 : rows], side)
             outbox[h, 0:DK, :] = (-moved[:, :DK]).astype(jnp.bfloat16)
             outbox[h, DK : 2 * DK, :] = moved[:, DK:].astype(jnp.bfloat16)
             kept = entry[rows - 1 : rows]
@@ -354,8 +415,7 @@
                 ),
             )
             outbox[h, 2 * DK : 2 * DK + META_ROWS, :] = meta.astype(jnp.bfloat16)
-        for member in range(share):
-            h = kh * share + member
+        for h, _ in overlaps:
 
             @pl.when(h != me)
             def _():
@@ -365,9 +425,18 @@
             def _():
                 inbox[me] = outbox[me]
 
+        for (h, parts), entry, mixing, side in zip(overlaps, entries, mixings, sides):
+            seen = mxu_wide(mixing * parts[4], side)
+            local[h] = seen[:, DK:]
+            reader[h] = entry * parts[0] - seen[:, :DK]
+
         return 0
 
-    lax.fori_loop(0, key_groups, key_group, 0)
+    lax.fori_loop(0, key_groups // together, some_heads, 0)
+
+    fetches[6].wait()
+    gate = gate_ref[...].astype(jnp.float32)
+    opened[...] = gate / (1.0 + jnp.exp(-gate))
 
     def state_copy(i):
         return pltpu.make_async_remote_copy(
@@ -438,13 +507,14 @@
         def _():
             landed(arrived, h, state_send, state_recv).wait_recv()
 
-        attention = local[h] + mxu(reader[h], arrived[h])
+    for h in range(heads):
+        at = slice(h * DV, (h + 1) * DV)
+        attention = local[h] + mxu_wide_left(reader[h], arrived[h])
         mean_square = jnp.mean(attention * attention, axis=-1, keepdims=True)
-        gate = gate_ref[:, h * DV : (h + 1) * DV].astype(jnp.float32)
-        gated = attention * lax.rsqrt(mean_square + norm_eps) * (gate / (1.0 + jnp.exp(-gate)))
-        normed[:, h * DV : (h + 1) * DV] = gated.astype(jnp.bfloat16)
-
-    fetch.wait()
+        gated = attention * lax.rsqrt(mean_square + norm_eps) * opened[:, at]
+        normed[:, at] = gated.astype(jnp.bfloat16)
+
+    weight_fetch.wait()
 
     def sum_copy(tile, away):
         peer = lax.rem(group + away, head_size)
@@ -529,17 +599,25 @@
     f32, bf16 = jnp.float32, jnp.bfloat16
     dma = pltpu.SemaphoreType.DMA
     vmem = pl.BlockSpec(memory_space=pltpu.VMEM)
+    hbm = pl.BlockSpec(memory_space=pltpu.HBM)
     return pl.pallas_call(
         functools.partial(layer_kernel, ctx_size, head_size),
         out_shape=(
             jax.ShapeDtypeStruct((own_rows, width), bf16),
             jax.ShapeDtypeStruct((heads, state_rows * DV), f32),
         ),
-        in_specs=[vmem] * 7
-        + [pl.BlockSpec(memory_space=pltpu.SMEM), pl.BlockSpec(memory_space=pl.ANY)],
+        in_specs=[hbm] * 7 + [pl.BlockSpec(memory_space=pltpu.SMEM), hbm],
         out_specs=(vmem, vmem),
         scratch_shapes=[
+            pltpu.VMEM(queries.shape, bf16),
+            pltpu.VMEM(keys.shape, bf16),
+            pltpu.VMEM(values.shape, bf16),
+            pltpu.VMEM(out_gate.shape, bf16),
+            pltpu.VMEM((heads, rows), f32),
+            pltpu.VMEM((heads, rows), f32),
+            pltpu.VMEM((1, rows), jnp.int32),
             pltpu.VMEM(out_weight.shape, bf16),
+            pltpu.VMEM((rows, heads * DV), f32),
             pltpu.VMEM((heads, rows, rows), f32),
             pltpu.VMEM((heads, rows, rows), f32),
             pltpu.VMEM((heads, 8, rows), f32),
@@ -548,13 +626,14 @@
             pltpu.VMEM((ctx_size, DK, DV), bf16),
             pltpu.VMEM((heads, DK, DV), bf16),
             pltpu.VMEM((heads, rows, DV), f32),
-            pltpu.VMEM((heads, rows, DK), bf16),
+            pltpu.VMEM((heads, rows, DK), f32),
             pltpu.VMEM((rows, heads * DV), bf16),
             pltpu.VMEM((DK, DV), f32),
             pltpu.VMEM((head_size * heads, state_rows, DV), f32),
             pltpu.VMEM((rows, width), f32),
             pltpu.VMEM((tiles, rows, COLUMN_TILE), bf16),
             pltpu.VMEM((tiles, head_size, own_rows, COLUMN_TILE), bf16),
+            dma((7,)),
             dma,
             dma((heads,)),
             dma((ctx_size,)),
@@ -568,15 +647,15 @@
             dma((tiles, head_size)),
         ],
         compiler_params=pltpu.CompilerParams(
-            collective_id=0, has_side_effects=True, vmem_limit_bytes=40 * 1024 * 1024
+            collective_id=0, has_side_effects=True, vmem_limit_bytes=56 * 1024 * 1024
         ),
     )(
         queries,
         keys,
         values,
         out_gate,
-        log_decay,
-        write_strength,
+        log_decay.T,
+        write_strength.T,
         segment_ids.reshape(1, rows),
         head_order,
         out_weight,

time: 52.6 us -> 43 us (0.82)
  the two profiles are of different devices: /device:TPU:31 before, /device:TPU:13 now
where the time goes in v2:
time: 43 us; the launch traced here: 42.8 us
  Pallas kernels  39.1 us (91%)
  local copies, waits for them, and re-layouts  3.04 us (7%)
  between operations  0.64 us (1%)
    pallas_call x1, Pallas kernels, head_owner(): pl.pallas_call(functools.partial(layer_kernel, ctx_size, head_size), out_...  39.1 us
    unnamed x2, local copies, waits for them, and re-layouts  3.04 us

profile of v2, /device:TPU:13, one launch (start us, length us, event | category | flops | bytes accessed | tf_op | source)
XLA Modules:
  0.0 42.8 jit_solution(11763660703592591649)
XLA Ops:
  0.6 39.1 %shard_map.104 = (bf16[32,2048]{1,0:T(8,128)(2,1)}, f32[8,2048]{1,0:T(8,128)}) custom-call(bf16[128,512]{1,0:T(8,128)(2,1)} %q_hbm.1, bf16[128,512]{1,0:T(8,128)(2,1)} %k_hbm.1, bf16[128,1024]{1,0:T(8,128)(2,1)} %v_hbm.1, bf16[128,1024]{1,0:T(8,128)(2,1)} %gate_hbm.1, f32[8,128]{1,0:T(8,128)} %bitcast.3, f32[8,128]{1,0:T(8,128)} %bitcast.4, ...), custom_call_target="tpu_custom_call" | custom-call | tf_op jit(solution)/shard_map/pallas_call | solution.py:603
  39.8 1.6 %copy.13 = bf16[32,2048]{1,0:T(8,128)(2,1)} copy(bf16[32,2048]{1,0:T(8,128)(2,1)} %get-tuple-element.4) | data formatting | bytes 262144
  41.3 1.5 %copy.14 = f32[8,2048]{1,0:T(8,128)} copy(f32[8,2048]{1,0:T(8,128)} %get-tuple-element.5) | data formatting | bytes 131072

commit v3 on v2

--- a/solution.py
+++ b/solution.py
@@ -216,14 +216,14 @@
     pairs = row_at // 2 == col_at // 2
     found = [eye - jnp.where(pairs, coupling, 0.0) for coupling in couplings]
     half = 2
-    while half < size:
+    while 2 * half < size:
         within = (row_at // (2 * half) == col_at // (2 * half)) & (row_at // half != col_at // half)
         below = [mxu(x, jnp.where(within, c, 0.0)) for x, c in zip(found, couplings)]
         found = [x - mxu(b, x) for x, b in zip(found, below)]
         half *= 2
     found = [x - eye for x in found]
     residue = [-x - c - mxu_wide(c, x) for x, c in zip(found, couplings)]
-    return [x + r + mxu(x, r) for x, r in zip(found, residue)]
+    return [x + r + mxu_wide(x, r) for x, r in zip(found, residue)]
 
 
 def layer_kernel(
@@ -262,6 +262,7 @@
     final,
     columns,
     partial,
+    paired,
     leaving,
     summands,
     fetch_sem,
@@ -274,6 +275,8 @@
     final_recv,
     column_send,
     column_recv,
+    mate_send,
+    mate_recv,
     sum_send,
     sum_recv,
 ):
@@ -357,7 +360,7 @@
 
     together = 2 if key_groups % 2 == 0 else 1
 
-    def some_heads(turn, _):
+    def some_heads(turn):
         overlaps = []
         for j in range(together):
             kh = lax.rem(me // share + 1 + turn * together + j, key_groups)
@@ -415,24 +418,21 @@
                 ),
             )
             outbox[h, 2 * DK : 2 * DK + META_ROWS, :] = meta.astype(jnp.bfloat16)
-        for h, _ in overlaps:
-
-            @pl.when(h != me)
-            def _():
-                map_copy(h).start()
-
-            @pl.when(h == me)
-            def _():
-                inbox[me] = outbox[me]
+        last_turn = turn == key_groups // together - 1
+        for h, _ in overlaps[: len(overlaps) - share if last_turn else None]:
+            map_copy(h).start()
+        if last_turn:
+            for away in range(1, share):
+                map_copy(me // share * share + lax.rem(me + away, share)).start()
+            inbox[me] = outbox[me]
 
         for (h, parts), entry, mixing, side in zip(overlaps, entries, mixings, sides):
             seen = mxu_wide(mixing * parts[4], side)
             local[h] = seen[:, DK:]
             reader[h] = entry * parts[0] - seen[:, :DK]
 
-        return 0
-
-    lax.fori_loop(0, key_groups // together, some_heads, 0)
+    for turn in range(key_groups // together):
+        some_heads(turn)
 
     fetches[6].wait()
     gate = gate_ref[...].astype(jnp.float32)
@@ -471,15 +471,22 @@
             state = jnp.where(meta[2:3] == doc_before, state, 0.0)
         doc_before = meta[3:4]
         state_low = state.astype(jnp.bfloat16)
-        entering[i] = state_low
-
-        @pl.when(me != i)
-        def _():
-            state_copy(i).start()
-
-        @pl.when(me == i)
-        def _():
-            arrived[i] = entering[i]
+        if i == 0:
+
+            @pl.when(me == 0)
+            def _():
+                arrived[...] = jnp.zeros_like(arrived)
+
+        else:
+            entering[i] = state_low
+
+            @pl.when(me != i)
+            def _():
+                state_copy(i).start()
+
+            @pl.when(me == i)
+            def _():
+                arrived[i] = entering[i]
 
         added = inbox[i, DK : 2 * DK, :].astype(jnp.float32)
         state = (meta[0:1] + meta[1:2]) * state + mxu(inbox[i, 0:DK, :], state_low) + added
@@ -503,7 +510,7 @@
 
     for h in range(heads):
 
-        @pl.when(me != h)
+        @pl.when((me != h) & (me != 0))
         def _():
             landed(arrived, h, state_send, state_recv).wait_recv()
 
@@ -516,24 +523,48 @@
 
     weight_fetch.wait()
 
+    half = head_size // 2
+    side, place_here = lax.rem(group, 2), group // 2
+    mate = 2 * place_here + 1 - side
+
+    def mate_copy(tile, place):
+        return pltpu.make_async_remote_copy(
+            src_ref=partial.at[tile, 2 * place + 1 - side],
+            dst_ref=paired.at[tile, place],
+            send_sem=mate_send.at[tile, place],
+            recv_sem=mate_recv.at[tile, place],
+            device_id=(me, mate),
+            device_id_type=MESH,
+        )
+
     def sum_copy(tile, away):
-        peer = lax.rem(group + away, head_size)
         return pltpu.make_async_remote_copy(
-            src_ref=leaving.at[tile, pl.ds(pl.multiple_of(peer * own_rows, own_rows), own_rows)],
+            src_ref=leaving.at[tile, away],
             dst_ref=summands.at[tile, away],
             send_sem=sum_send.at[tile, away],
             recv_sem=sum_recv.at[tile, away],
-            device_id=(me, peer),
+            device_id=(me, 2 * lax.rem(place_here + away, half) + side),
             device_id_type=MESH,
         )
+
+    def pass_on(tile):
+        for place in range(half):
+            mate_copy(tile, place).wait_recv()
+        for away in range(1, half):
+            place = lax.rem(place_here + away, half)
+            pair_sum = partial[tile, 2 * place + side] + paired[tile, place]
+            leaving[tile, away] = pair_sum.astype(jnp.bfloat16)
+            sum_copy(tile, away).start()
 
     for tile in range(tiles):
         at = slice(tile * COLUMN_TILE, (tile + 1) * COLUMN_TILE)
         product_here = jnp.dot(normed[...], weight[:, at], preferred_element_type=jnp.float32)
-        partial[:, at] = product_here
-        leaving[tile] = product_here.astype(jnp.bfloat16)
-        for away in range(1, head_size):
-            sum_copy(tile, away).start()
+        partial[tile] = product_here.reshape(head_size, own_rows, COLUMN_TILE)
+        for place in range(half):
+            mate_copy(tile, place).start()
+        if tile > 0:
+            pass_on(tile - 1)
+    pass_on(tiles - 1)
 
     for away in range(1, ctx_size):
         source = lax.rem(me + away, ctx_size)
@@ -561,8 +592,8 @@
 
     for tile in range(tiles):
         at = slice(tile * COLUMN_TILE, (tile + 1) * COLUMN_TILE)
-        total = partial[pl.ds(pl.multiple_of(group * own_rows, own_rows), own_rows), at]
-        for away in range(1, head_size):
+        total = partial[tile, group] + paired[tile, place_here]
+        for away in range(1, half):
             sum_copy(tile, away).wait_recv()
             total = total + summands[tile, away].astype(jnp.float32)
         out_ref[:, at] = total.astype(jnp.bfloat16)
@@ -578,11 +609,19 @@
     for away in range(1, ctx_size):
         other = lax.rem(me + away, ctx_size)
         map_copy(other).wait_send()
-        state_copy(other).wait_send()
         final_copy(other).wait_send()
+    for i in range(1, ctx_size):
+
+        @pl.when(me != i)
+        def _():
+            state_copy(i).wait_send()
+
     for away in range(1, head_size):
         column_copy(lax.rem(group + away, head_size), group, away).wait_send()
-        for tile in range(tiles):
+    for tile in range(tiles):
+        for place in range(half):
+            mate_copy(tile, place).wait_send()
+        for away in range(1, half):
             sum_copy(tile, away).wait_send()
 
 
@@ -595,6 +634,7 @@
     width = out_weight.shape[1]
     tiles = width // COLUMN_TILE
     own_rows = rows // head_size
+    half = head_size // 2
     state_rows = DK // ctx_size
     f32, bf16 = jnp.float32, jnp.bfloat16
     dma = pltpu.SemaphoreType.DMA
@@ -630,9 +670,10 @@
             pltpu.VMEM((rows, heads * DV), bf16),
             pltpu.VMEM((DK, DV), f32),
             pltpu.VMEM((head_size * heads, state_rows, DV), f32),
-            pltpu.VMEM((rows, width), f32),
-            pltpu.VMEM((tiles, rows, COLUMN_TILE), bf16),
-            pltpu.VMEM((tiles, head_size, own_rows, COLUMN_TILE), bf16),
+            pltpu.VMEM((tiles, head_size, own_rows, COLUMN_TILE), f32),
+            pltpu.VMEM((tiles, half, own_rows, COLUMN_TILE), f32),
+            pltpu.VMEM((tiles, half, own_rows, COLUMN_TILE), bf16),
+            pltpu.VMEM((tiles, half, own_rows, COLUMN_TILE), bf16),
             dma((7,)),
             dma,
             dma((heads,)),
@@ -643,8 +684,10 @@
             dma((ctx_size,)),
             dma((head_size,)),
             dma((head_size,)),
-            dma((tiles, head_size)),
-            dma((tiles, head_size)),
+            dma((tiles, half)),
+            dma((tiles, half)),
+            dma((tiles, half)),
+            dma((tiles, half)),
         ],
         compiler_params=pltpu.CompilerParams(
             collective_id=0, has_side_effects=True, vmem_limit_bytes=56 * 1024 * 1024
@@ -664,7 +707,11 @@
 
 def per_device(queries, keys, values, *rest):
     heads = values.shape[1] // DV
-    one_owner_per_head = heads == lax.axis_size("ctx") and queries.shape[0] == DK
+    one_owner_per_head = (
+        heads == lax.axis_size("ctx")
+        and queries.shape[0] == DK
+        and lax.axis_size("head") % 2 == 0
+    )
     form = head_owner if one_owner_per_head else gathered_prefix
     return form(queries, keys, values, *rest)
 

time: 43 us -> 44.3 us (1.030); the launches traced: 42.8 us -> 43.5 us
  Pallas kernels: 39.1 us -> 39.8 us
    pallas_call x1, Pallas kernels: 39.1 us -> 39.8 us  [head_owner(): pl.pallas_call(functools.partial(layer_kernel, ctx_size, head_size), out_...]
where the time goes in v3:
time: 44.3 us; the launch traced here: 43.5 us
  Pallas kernels  39.8 us (90%)
  local copies, waits for them, and re-layouts  3.04 us (7%)
  between operations  0.64 us (1%)
    pallas_call x1, Pallas kernels, head_owner(): pl.pallas_call(functools.partial(layer_kernel, ctx_size, head_size), out_...  39.8 us
    unnamed x2, local copies, waits for them, and re-layouts  3.04 us

profile of v3, /device:TPU:13, one launch (start us, length us, event | category | flops | bytes accessed | tf_op | source)
XLA Modules:
  0.0 43.5 jit_solution(12742306568134368550)
XLA Ops:
  0.6 39.8 %shard_map.104 = (bf16[32,2048]{1,0:T(8,128)(2,1)}, f32[8,2048]{1,0:T(8,128)}) custom-call(bf16[128,512]{1,0:T(8,128)(2,1)} %q_hbm.1, bf16[128,512]{1,0:T(8,128)(2,1)} %k_hbm.1, bf16[128,1024]{1,0:T(8,128)(2,1)} %v_hbm.1, bf16[128,1024]{1,0:T(8,128)(2,1)} %gate_hbm.1, f32[8,128]{1,0:T(8,128)} %bitcast.3, f32[8,128]{1,0:T(8,128)} %bitcast.4, ...), custom_call_target="tpu_custom_call" | custom-call | tf_op jit(solution)/shard_map/pallas_call | solution.py:643
  40.4 1.6 %copy.13 = bf16[32,2048]{1,0:T(8,128)(2,1)} copy(bf16[32,2048]{1,0:T(8,128)(2,1)} %get-tuple-element.4) | data formatting | bytes 262144
  42.0 1.5 %copy.14 = f32[8,2048]{1,0:T(8,128)} copy(f32[8,2048]{1,0:T(8,128)} %get-tuple-element.5) | data formatting | bytes 131072
